TPU v7x, 512 devices: a whole 4x4x16 slice. The times are simulated.
512 devices in a mesh: ctx: 32 (over z_lo, x), head: 4 (over z_hi, core), qry: 4 (over y).
Axes of the slice: x: 4, y: 4, z: 16 (z_hi: 2, z_lo: 8; z = z_hi * 8 + z_lo), core: 2. Of those that a mesh axis runs over, the one named last changes fastest.
Arguments:
- queries: bfloat16 [4096, 4, 896], P(('qry', 'ctx'), 'head'), may hold values from -110 to 110
- key_cache: bfloat16 [4, 8192, 128], P('head', 'ctx'), may hold values from -4 to 4
- key_positions: int32 [8192], P('ctx'), may hold values from 0 to 8191, each once
- span_end: int32 [4096], P(('qry', 'ctx')), may hold values from 2048 to 8192, as said below
Outputs:
- importance: float32 [4, 8192], P('head', 'ctx')
Inputs may be any that keep to these rules, and one draw needn't show every extreme that they name: `span_end`: constant over each of 16 runs of 256 consecutive queries, nondecreasing; the first run ends at 2048, the last at 8192.
All inputs are finite; a program needn't handle non-finite values.
Results may differ from a plain program's by a relative error of at most 0.0003.
Values may be sent and summed in bfloat16 or wider, within the bound.
A program may use at most 64 MiB of HBM per device.

v0:
```python
import jax
import jax.numpy as jnp
from jax import lax
from jax.sharding import PartitionSpec as P

NEG_FILL = -1e30


def shards(queries, key_cache, key_positions, span_end):
    key_rows = key_cache[0]
    head_width = key_rows.shape[1]
    group_size = queries.shape[2] // head_width
    score_scale = head_width ** (-0.5)

    def score_tile(query_rows, member, keys_part):
        part = query_rows[:, 0, member * head_width : (member + 1) * head_width]
        return (
            jnp.einsum("qd,kd->qk", part, keys_part, preferred_element_type=jnp.float32)
            * score_scale
        )

    piece = (
        lax.all_gather(queries, "ctx", axis=0, tiled=True),
        lax.all_gather(span_end, "ctx", axis=0, tiled=True),
    )
    query_rows = piece[0]
    visible = key_positions[None, :] < piece[1][:, None]
    peak_list = []
    mass_list = []
    for member in range(group_size):
        masked = jnp.where(visible, score_tile(query_rows, member, key_rows), NEG_FILL)
        top = jnp.max(masked, axis=1)
        peak_list.append(top)
        mass_list.append(jnp.sum(jnp.where(visible, jnp.exp(masked - top[:, None]), 0.0), axis=1))
    peaks = jnp.stack(peak_list, 1)
    masses = jnp.stack(mass_list, 1)
    global_top = lax.pmax(peaks, "ctx")
    masses = lax.psum(masses * jnp.exp(peaks - global_top), "ctx")
    peaks = global_top
    log_totals = peaks + jnp.log(masses)
    initial_best = jnp.full((key_rows.shape[0],), NEG_FILL, jnp.float32)
    piece = (
        lax.all_gather(queries, "ctx", axis=0, tiled=True),
        lax.all_gather(span_end, "ctx", axis=0, tiled=True),
    )
    query_rows = piece[0]
    visible = key_positions[None, :] < piece[1][:, None]
    result = jnp.full((key_rows.shape[0],), NEG_FILL, jnp.float32)
    for member in range(group_size):
        scores = score_tile(query_rows, member, key_rows)
        shifted = jnp.where(visible, scores - log_totals[:, member : member + 1], NEG_FILL)
        result = jnp.maximum(result, jnp.max(shifted, axis=0))
    local_best = jnp.maximum(initial_best, result)
    importance = lax.pmax(local_best, "qry")
    return importance[None, :]


def solution(mesh):
    placed = (P(("qry", "ctx"), "head", None), P("head", "ctx", None), P("ctx"), P(("qry", "ctx")))
    return jax.shard_map(
        shards, mesh=mesh, in_specs=placed, out_specs=P("head", "ctx"), check_vma=False
    )
```

profile of v0, /device:TPU:8, one launch (start us, length us, event | category | flops | bytes accessed | tf_op | source)
XLA Modules:
  0.0 721.4 jit_solution(657895573492430902)
XLA Ops:
  6.5 0.0 copy-start
  6.5 0.0 all-gather.2.cloned.1.call-start
  6.5 0.7 all-gather.2.cloned.1.call-update
  7.3 1.3 dynamic-slice
  9.2 0.9 dynamic-update-slice
  10.1 26.1 %all-reduce = s32[1024]{0:T(1024)S(1)} all-reduce(s32[1024]{0:T(1024)S(1)} %dynamic-update-slice), channel_id=1, replica_groups=mesh['ctx'=32,'head'=4,'qry'=4] {'ctx'}, use_global_device_ids=true, to_apply=%add | all-reduce | flops 1024 | bytes 8192
  36.1 201.3 %all-gather.2.cloned.1.call-done = bf16[1024,1,896]{2,0,1:T(8,128)(2,1)} async-done(((bf16[32,1,896]{2,0,1:T(8,128)(2,1)}), bf16[1024,1,896]{2,0,1:T(8,128)(2,1)}) %all-gather.2.cloned.1.call-update) | async-done | bytes 1835024 | tf_op jit(solution)/shard_map/all_gather | solution.py:43
  237.5 0.0 copy-done
  237.5 1.4 convolution_multiply_fusion.1
  238.8 1.2 convolution_multiply_fusion.2
  240.1 0.3 convolution_multiply_fusion.3
  240.4 0.0 copy-start.6
  240.4 0.3 convolution_multiply_fusion.4
  240.7 0.3 convolution_multiply_fusion.5
  241.1 0.3 convolution_multiply_fusion.6
  241.4 0.8 fusion.20
  242.2 0.2 copy-done.3
  242.4 1.6 fusion.6
  244.0 0.1 stack.55
  244.0 233.8 %pmax.14 = f32[1024,7]{0,1:T(8,128)S(1)} all-reduce(f32[1024,7]{0,1:T(8,128)S(1)} %stack.55), channel_id=1, replica_groups=mesh['ctx'=32,'head'=4,'qry'=4] {'ctx'}, use_global_device_ids=true, to_apply=%region_7.8 | all-reduce | flops 7168 | bytes 57344 | tf_op jit(solution)/shard_map/pmax | solution.py:37
  477.9 0.1 stack.63
  477.9 224.0 %psum.7 = f32[1024,7]{0,1:T(8,128)S(1)} all-reduce(f32[1024,7]{0,1:T(8,128)S(1)} %exponential_multiply_fusion), channel_id=1, replica_groups=mesh['ctx'=32,'head'=4,'qry'=4] {'ctx'}, use_global_device_ids=true, to_apply=%region_15.16 | all-reduce | flops 7168 | bytes 57344 | tf_op jit(solution)/shard_map/psum | solution.py:38
  702.0 3.5 fusion.7
  705.4 9.2 %pmax.15 = f32[1,256]{1,0:T(1,128)} all-reduce(f32[1,256]{1,0:T(1,128)S(1)} %bitcast.84), channel_id=1, replica_groups=mesh['ctx'=32,'head'=4,'qry'=4] {'qry'}, use_global_device_ids=true, to_apply=%region_23.24 | all-reduce | flops 256 | bytes 2048 | tf_op jit(solution)/shard_map/pmax | solution.py:54
  (15 shorter events, 0.1 us)
Async XLA Ops:
  6.5 230.9 %copy-start = (bf16[1,256,128]{2,1,0:T(8,128)(2,1)S(1)}, bf16[1,256,128]{2,1,0:T(8,128)(2,1)}, u32[]{:S(2)}) copy-start(bf16[1,256,128]{2,1,0:T(8,128)(2,1)} %param.5) | copy-start | bytes 196612
  6.5 230.9 %all-gather.2.cloned.1.call-start = ((), (), s32[]{:S(2)}) async-start(), calls=%async_computation | async-start | bytes 1892352 | tf_op jit(solution)/shard_map/all_gather | solution.py:43
  237.5 2.6 copy-start.5
  240.4 1.0 copy-start.6
  240.7 1.5 copy-start.1
  241.0 1.2 copy-start.2
  241.4 1.0 copy-start.3
  242.2 1.8 copy-start.4
Sparse Core Ops, SparseCore 0:
  9.4 227.9 all-gather.1
where the time goes:
time: 722 us; the launch traced here: 721 us
  blocking collectives  493 us (68%)
  waiting for transfers between devices  202 us (28%)
  between operations  14.2 us (2%)
    pmax x1, blocking collectives, shards(): global_top = lax.pmax(peaks, 'ctx')  234 us
    psum x1, blocking collectives, shards(): masses = lax.psum(masses * jnp.exp(peaks - global_top), 'ctx')  224 us
    all_gather x1, waiting for transfers between devices, shards(): lax.all_gather(queries, 'ctx', axis=0, tiled=True)  201 us
    unnamed x1, blocking collectives  26.1 us
  transfers between devices with their start and end apart: 1, of which 1 were waited for; matrix products, arithmetic and copies ran while one was open for 0% of the time, Pallas kernels for 0%

commit v1 on v0

v1 whole, which is shorter than its diff:
```python
import functools
import math

import jax
import jax.numpy as jnp
from jax import lax
from jax.experimental import pallas as pl
from jax.experimental.pallas import tpu as pltpu
from jax.sharding import PartitionSpec as P

NEG_FILL = -1e30
MESH = pl.DeviceIdType.MESH
NX, NY, NZ = 4, 4, 8
PAIRS = NZ // 2


def kernel(group, q_ref, k_ref, p_ref, e_ref, o_ref, qbuf, kbuf, pbuf, ebuf, sbuf, mst, lst, colb, st, cm, rbuf,
           loc, qs, qr, kr, pr, ks, ps, yr, ys, ss, sr, cs, cr):
    ctx, y = lax.axis_index("ctx"), lax.axis_index("qry")
    z, x = ctx // NX, lax.rem(ctx, NX)
    keys, width = k_ref.shape
    quarter = keys // NY
    rows = qbuf.shape[0] * qbuf.shape[1]
    scale = width**-0.5
    to_exp2 = math.log2(math.e) * scale
    mine = pl.ds(pl.multiple_of(y * quarter, quarter), quarter)

    def xdev(d):
        return {"ctx": z * NX + lax.rem(x + d, NX)}

    def ydev(d):
        return {"qry": lax.rem(y + d, NY)}

    def zdev(target):
        return {"ctx": target * NX + x}

    def remote(src, dst, send, recv, dev):
        return pltpu.make_async_remote_copy(src_ref=src, dst_ref=dst, send_sem=send, recv_sem=recv, device_id=dev, device_id_type=MESH)

    def drain(ref, sem):
        pltpu.make_async_copy(ref, ref, sem).wait()

    barrier = pltpu.get_barrier_semaphore()

    def greet(dev):
        pl.semaphore_signal(barrier, inc=1, device_id=dev, device_id_type=MESH)

    @pl.when(z > 0)
    def _():
        greet(zdev(z - 1))

    @pl.when(z < NZ - 1)
    def _():
        greet(zdev(z + 1))

    for d in (1, 3, 2):
        greet(xdev(d))
        greet(ydev(d))

    local = [
        pltpu.make_async_copy(k_ref.at[mine], kbuf.at[z, mine], loc.at[0]),
        pltpu.make_async_copy(p_ref, pbuf.at[z], loc.at[1]),
        pltpu.make_async_copy(q_ref, qbuf.at[x], loc.at[2]),
        pltpu.make_async_copy(e_ref, ebuf, loc.at[3]),
    ]
    for c in local:
        c.start()
    mst[...] = jnp.full(mst.shape, NEG_FILL, jnp.float32)
    lst[...] = jnp.zeros(lst.shape, jnp.float32)
    st[x] = jnp.zeros(st.shape[1:], jnp.float32)
    ends = jnp.where((z > 0) & (z < NZ - 1), 2, 1)
    pl.semaphore_wait(barrier, ends + 6)

    def send_block(src_k, src_p, block, target):
        remote(src_k, kbuf.at[block, mine], ks.at[0], kr.at[block], zdev(target)).start()
        remote(src_p, pbuf.at[block], ps.at[0], pr.at[block], zdev(target)).start()

    def wait_block(block):
        drain(kbuf.at[block, mine], kr.at[block])
        drain(pbuf.at[block], pr.at[block])

    def fan_out(g):
        part = kbuf.at[pl.ds(2 * g, 2), mine]
        for d in (1, 3, 2):
            remote(part, part, ys.at[0], yr.at[g], ydev(d)).start()

    for i in range(NZ):

        @pl.when((z == i) & (z < NZ - 1))
        def _():
            send_block(k_ref.at[mine], p_ref, z, z + 1)

        @pl.when(z > i)
        def _():
            wait_block(i)

            @pl.when(z < NZ - 1)
            def _():
                send_block(kbuf.at[i, mine], pbuf.at[i], i, z + 1)

        if i == 0:
            for j in range(NZ - 1):

                @pl.when(z > j)
                def _():
                    send_block(k_ref.at[mine], p_ref, z, j)

            for d in (1, 3, 2):
                remote(q_ref, qbuf.at[x], qs.at[0], qr.at[0], xdev(d)).start()
            local[0].wait()
            local[1].wait()

        if i % 2:

            @pl.when(z >= i)
            def _():
                fan_out(i // 2)

    def late(g):
        @pl.when(z < 2 * g)
        def _():
            wait_block(2 * g)

        @pl.when(z < 2 * g + 1)
        def _():
            wait_block(2 * g + 1)
            fan_out(g)

    late(0)
    local[2].wait()
    local[3].wait()
    drain(qbuf.at[pl.ds(0, NX - 1)], qr.at[0])
    end = ebuf[0:1, 0:1]

    def bias_of(g):
        pos = jnp.concatenate([pbuf[2 * g], pbuf[2 * g + 1]], axis=1)
        return jnp.where(pos < end, 0.0, NEG_FILL)

    def scan_pair(g, unused):
        @pl.when(g < PAIRS - 1)
        def _():
            late(g + 1)

        drain(kbuf.at[pl.ds(0, 2), pl.ds(0, (NY - 1) * quarter)], yr.at[g])
        part = kbuf[pl.ds(2 * g, 2)].reshape(2 * keys, width)
        bias = bias_of(g)
        for m in range(group):
            qm = qbuf[:, :, m * width : (m + 1) * width].reshape(rows, width)
            s = lax.dot_general(qm, part, (((1,), (1,)), ((), ())), preferred_element_type=jnp.float32)
            sbuf[g, m] = s
            t = s + bias
            pieces = [t[:, c * 128 : (c + 1) * 128] for c in range(2 * keys // 128)]
            old = mst[m]
            new = functools.reduce(jnp.maximum, pieces, old)
            total = lst[m] * jnp.exp2((old - new) * to_exp2)
            for piece in pieces:
                total = total + jnp.exp2((piece - new) * to_exp2)
            mst[m] = new
            lst[m] = total
        return unused

    lax.fori_loop(0, PAIRS, scan_pair, 0)

    eye = lax.broadcasted_iota(jnp.int32, (rows, 128), 0) == lax.broadcasted_iota(jnp.int32, (rows, 128), 1)
    for m in range(group):
        tops = mst[m]
        top = jnp.max(tops, axis=1, keepdims=True)
        mass = jnp.sum(lst[m] * jnp.exp2((tops - top) * to_exp2), axis=1, keepdims=True)
        st[x, m : m + 1] = jnp.sum(jnp.where(eye, top, 0.0), axis=0, keepdims=True)
        st[x, 8 + m : 9 + m] = jnp.sum(jnp.where(eye, mass, 0.0), axis=0, keepdims=True)
    for d in (1, 3, 2):
        remote(st.at[x], st.at[x], ss.at[0], sr.at[0], xdev(d)).start()
    drain(st.at[pl.ds(0, NX - 1)], sr.at[0])
    tops, masses = st[:, 0:8], st[:, 8:16]
    top = jnp.max(tops, axis=0)
    mass = jnp.sum(masses * jnp.exp2((tops - top[None]) * to_exp2), axis=0)
    total = top + jnp.log(mass) * (1.0 / scale)
    for m in range(group):
        col = jnp.sum(jnp.where(eye, total[m : m + 1], 0.0), axis=1, keepdims=True)
        colb[m] = jnp.broadcast_to(col, (rows, 128))

    def best_pair(g, unused):
        def member(m, acc):
            for r in range(rows // 8):
                col = colb[m, r * 8 : (r + 1) * 8]
                acc = tuple(
                    jnp.maximum(a, sbuf[g, m, r * 8 : (r + 1) * 8, c * 128 : (c + 1) * 128] - col)
                    for c, a in enumerate(acc)
                )
            return acc

        start = tuple(jnp.full((8, 128), NEG_FILL, jnp.float32) for c in range(2 * keys // 128))
        acc = lax.fori_loop(0, group, member, start)
        best = jnp.concatenate([jnp.max(a, axis=0, keepdims=True) for a in acc], axis=1) * scale
        best = jnp.where(bias_of(g) < 0.0, NEG_FILL, best)
        cm[2 * g] = best[:, :keys]
        cm[2 * g + 1] = best[:, keys:]
        return unused

    lax.fori_loop(0, PAIRS, best_pair, 0)

    def owner(step, unused):
        far_z = lax.rem(z + step // NY, NZ)
        far_y = lax.rem(y + lax.rem(step, NY), NY)
        remote(cm.at[far_z], rbuf.at[z * NY + y], cs.at[0], cr.at[0], {"ctx": far_z * NX + x, "qry": far_y}).start()
        return unused

    lax.fori_loop(1, NZ * NY, owner, 0)
    rbuf[z * NY + y] = cm[z]
    drain(rbuf.at[pl.ds(0, NZ * NY - 1)], cr.at[0])
    o_ref[...] = jnp.max(rbuf[...], axis=0)

    drain(rbuf.at[pl.ds(0, NZ * NY - 1)], cs.at[0])
    drain(st.at[pl.ds(0, NX - 1)], ss.at[0])
    drain(qbuf.at[pl.ds(0, NX - 1)], qs.at[0])
    drain(kbuf.at[pl.ds(0, 6)], ys.at[0])
    for v in range(NZ):
        count = 2 * v + 1 if v < NZ - 1 else v

        @pl.when(z == v)
        def _():
            drain(sbuf.at[0, 0, pl.ds(0, count * 8)], ks.at[0])
            drain(rbuf.at[pl.ds(0, count)], ps.at[0])


def shards(queries, key_cache, key_positions, span_end):
    own, unused, lanes = queries.shape
    keys, width = key_cache.shape[1:]
    group = lanes // width
    rows = own * NX
    dma = lambda n: pltpu.SemaphoreType.DMA((n,))
    return pl.pallas_call(
        functools.partial(kernel, group),
        out_shape=jax.ShapeDtypeStruct((1, keys), jnp.float32),
        in_specs=[pl.BlockSpec(memory_space=pl.ANY)] * 4,
        out_specs=pl.BlockSpec(memory_space=pltpu.VMEM),
        scratch_shapes=[
            pltpu.VMEM((NX, own, lanes), jnp.bfloat16),
            pltpu.VMEM((NZ, keys, width), jnp.bfloat16),
            pltpu.VMEM((NZ, 1, keys), jnp.int32),
            pltpu.VMEM((1, own), jnp.int32),
            pltpu.VMEM((PAIRS, group, rows, 2 * keys), jnp.float32),
            pltpu.VMEM((group, rows, 128), jnp.float32),
            pltpu.VMEM((group, rows, 128), jnp.float32),
            pltpu.VMEM((group, rows, 128), jnp.float32),
            pltpu.VMEM((NX, 16, 128), jnp.float32),
            pltpu.VMEM((NZ, 1, keys), jnp.float32),
            pltpu.VMEM((NZ * NY, 1, keys), jnp.float32),
            dma(4), dma(1), dma(1), dma(NZ), dma(NZ), dma(1), dma(1), dma(PAIRS), dma(1), dma(1), dma(1), dma(1), dma(1),
        ],
        compiler_params=pltpu.CompilerParams(collective_id=0, has_side_effects=True, vmem_limit_bytes=58 << 20),
    )(queries[:, 0], key_cache[0], key_positions[None], span_end[None])


def solution(mesh):
    placed = (P(("qry", "ctx"), "head", None), P("head", "ctx", None), P("ctx"), P(("qry", "ctx")))
    return jax.shard_map(shards, mesh=mesh, in_specs=placed, out_specs=P("head", "ctx"), check_vma=False)
```

time: 722 us -> 51.9 us (0.07)
  the two profiles are of different devices: /device:TPU:8 before, /device:TPU:480 now
where the time goes in v1:
time: 51.9 us; the launch traced here: 51.7 us
  Pallas kernels  50.5 us (97%)
  local copies, waits for them, and re-layouts  1.24 us (2%)
    pallas_call x1, Pallas kernels, shards(): pl.pallas_call(functools.partial(kernel, group), out_shape=jax.ShapeDtype...  50.5 us
    unnamed x1, local copies, waits for them, and re-layouts  1.24 us

profile of v1, /device:TPU:480, one launch (start us, length us, event | category | flops | bytes accessed | tf_op | source)
XLA Modules:
  0.0 51.7 jit_solution(8759012476187833736)
XLA Ops:
  0.0 50.5 %shard_map.46 = f32[1,256]{1,0:T(1,128)} custom-call(bf16[32,896]{1,0:T(8,128)(2,1)} %bitcast.5, bf16[256,128]{1,0:T(8,128)(2,1)} %bitcast.4, s32[1,256]{1,0:T(1,128)} %bitcast.6, s32[1,32]{1,0:T(1,128)} %bitcast.7), custom_call_target="tpu_custom_call" | custom-call | tf_op jit(solution)/shard_map/pallas_call | solution.py:232
  50.5 1.2 %copy.6 = f32[1,256]{1,0:T(1,128)} copy(f32[1,256]{1,0:T(1,128)} %shard_map.46) | data formatting | bytes 2048

commit v2 on v1

v2 whole, which is shorter than its diff:
```python
import functools
import math

import jax
import jax.numpy as jnp
from jax import lax
from jax.experimental import pallas as pl
from jax.experimental.pallas import tpu as pltpu
from jax.sharding import PartitionSpec as P

NEG_FILL = -1e30
MESH = pl.DeviceIdType.MESH
NX, NY, NZ = 4, 4, 8
HALF = NZ // 2


def kernel(group, q_ref, k_ref, p_ref, e_ref, o_ref, qbuf, kbuf, pbuf, ebuf, sbuf, mst, lst, colb, st, cm, rbuf,
           lq, le, qr, qz, qs, kr, pr, ks, ps, yr, ys, ss, sr, cs, cr):
    ctx, y = lax.axis_index("ctx"), lax.axis_index("qry")
    z, x = ctx // NX, lax.rem(ctx, NX)
    side = lax.rem(z, 2)
    twin = z + 1 - 2 * side
    half = z // HALF
    inside = side == half
    keys, width = k_ref.shape
    quarter = keys // NY
    rows = 2 * qbuf.shape[1] * qbuf.shape[2]
    scale = width**-0.5
    to_exp2 = math.log2(math.e) * scale
    mine = pl.ds(pl.multiple_of(y * quarter, quarter), quarter)

    def at(zz, xx):
        return {"ctx": zz * NX + xx}

    def turn(v, d):
        return lax.rem(v + d, 4)

    def remote(src, dst, send, recv, dev):
        return pltpu.make_async_remote_copy(src_ref=src, dst_ref=dst, send_sem=send, recv_sem=recv, device_id=dev, device_id_type=MESH)

    def drain(ref, sem):
        pltpu.make_async_copy(ref, ref, sem).wait()

    barrier = pltpu.get_barrier_semaphore()

    def greet(dev):
        pl.semaphore_signal(barrier, inc=1, device_id=dev, device_id_type=MESH)

    for j in range(HALF):
        source = HALF * side + j

        @pl.when(source != z)
        def _():
            greet(at(source, x))

    for d in (1, 3, 2):
        greet({"qry": turn(y, d)})
        greet(at(z, turn(x, d)))
    greet(at(twin, x))

    pltpu.make_async_copy(q_ref, qbuf.at[side, x], lq.at[0]).start()
    pltpu.make_async_copy(e_ref, ebuf, le.at[0]).start()
    slot = lax.rem(z, HALF)

    @pl.when(inside)
    def _():
        pltpu.make_async_copy(k_ref.at[mine], kbuf.at[y, slot], kr.at[slot // 2]).start()
        pltpu.make_async_copy(p_ref, pbuf.at[slot], pr.at[0]).start()

    mst[...] = jnp.full(mst.shape, NEG_FILL, jnp.float32)
    lst[...] = jnp.zeros(lst.shape, jnp.float32)
    st[side, x] = jnp.zeros(st.shape[2:], jnp.float32)
    pl.semaphore_wait(barrier, jnp.where(inside, 10, 11))

    remote(q_ref, qbuf.at[side, x], qs.at[0], qz.at[0], at(twin, x)).start()
    for i in range(HALF):
        target = 2 * i + half

        @pl.when(target != z)
        def _():
            remote(k_ref.at[mine], kbuf.at[y, slot], ks.at[0], kr.at[slot // 2], at(target, x)).start()
            remote(p_ref, pbuf.at[slot], ps.at[0], pr.at[0], at(target, x)).start()

    for d in (1, 3, 2):
        remote(q_ref, qbuf.at[side, x], qs.at[0], qr.at[0], at(z, turn(x, d))).start()
    drain(qbuf.at[0, 0], qz.at[0])
    passed = qbuf.at[1 - side, x]
    for d in (1, 3, 2):
        remote(passed, passed, qs.at[0], qr.at[1], at(z, turn(x, d))).start()

    def fan_out(g):
        drain(kbuf.at[0, pl.ds(0, 2)], kr.at[g])
        part = kbuf.at[y, pl.ds(2 * g, 2)]
        for d in (1, 3, 2):
            remote(part, part, ys.at[0], yr.at[g], {"qry": turn(y, d)}).start()

    fan_out(0)
    drain(q_ref, lq.at[0])
    drain(e_ref, le.at[0])
    drain(qbuf.at[0, pl.ds(0, NX - 1)], qr.at[0])
    drain(qbuf.at[0, pl.ds(0, NX - 1)], qr.at[1])
    drain(pbuf, pr.at[0])
    end = ebuf[0:1, 0:1]

    def bias_of(g):
        pos = jnp.concatenate([pbuf[2 * g], pbuf[2 * g + 1]], axis=1)
        return jnp.where(pos < end, 0.0, NEG_FILL)

    def scan_pair(g, unused):
        @pl.when(g < 1)
        def _():
            fan_out(g + 1)

        drain(kbuf.at[pl.ds(0, NY - 1), pl.ds(0, 2)], yr.at[g])
        parts = [kbuf[:, 2 * g + j].reshape(keys, width) for j in range(2)]
        bias = bias_of(g)
        for m in range(group):
            qm = qbuf[:, :, :, m * width : (m + 1) * width].reshape(rows, width)
            pieces = []
            for j, part in enumerate(parts):
                s = lax.dot_general(qm, part, (((1,), (1,)), ((), ())), preferred_element_type=jnp.float32)
                sbuf[g, m, :, j * keys : (j + 1) * keys] = s
                t = s + bias[:, j * keys : (j + 1) * keys]
                pieces += [t[:, c * 128 : (c + 1) * 128] for c in range(keys // 128)]
            old = mst[m]
            new = functools.reduce(jnp.maximum, pieces, old)
            total = lst[m] * jnp.exp2((old - new) * to_exp2)
            for piece in pieces:
                total = total + jnp.exp2((piece - new) * to_exp2)
            mst[m] = new
            lst[m] = total
        return unused

    lax.fori_loop(0, 2, scan_pair, 0)

    eye = lax.broadcasted_iota(jnp.int32, (128, 128), 0) == lax.broadcasted_iota(jnp.int32, (128, 128), 1)
    for m in range(group):
        for b in range(rows // 128):
            tops = mst[m, b * 128 : (b + 1) * 128]
            top = jnp.max(tops, axis=1, keepdims=True)
            mass = jnp.sum(lst[m, b * 128 : (b + 1) * 128] * jnp.exp2((tops - top) * to_exp2), axis=1, keepdims=True)
            r = m * (rows // 128) + b
            st[side, x, 0, r : r + 1] = jnp.sum(jnp.where(eye, top, 0.0), axis=0, keepdims=True)
            st[side, x, 1, r : r + 1] = jnp.sum(jnp.where(eye, mass, 0.0), axis=0, keepdims=True)
    own = st.at[side, x]
    for zz in (twin, z):
        for d in (2, 1, 3):
            remote(own, own, ss.at[0], sr.at[0], at(zz, turn(x, d))).start()
    remote(own, own, ss.at[0], sr.at[0], at(twin, x)).start()

    drain(sbuf.at[0, 0, pl.ds(0, 56)], sr.at[0])
    tops = [st[e, i, 0] for e in range(2) for i in range(NX)]
    masses = [st[e, i, 1] for e in range(2) for i in range(NX)]
    top = functools.reduce(jnp.maximum, tops)
    mass = sum(b * jnp.exp2((a - top) * to_exp2) for a, b in zip(tops, masses))
    total = top + jnp.log(mass) * (1.0 / scale)
    for m in range(group):
        for b in range(rows // 128):
            r = m * (rows // 128) + b
            col = jnp.sum(jnp.where(eye, total[r : r + 1], 0.0), axis=1, keepdims=True)
            colb[m, b * 128 : (b + 1) * 128] = jnp.broadcast_to(col, (128, 128))

    def best_pair(g, unused):
        def member(m, acc):
            for r in range(rows // 8):
                col = colb[m, r * 8 : (r + 1) * 8]
                acc = tuple(
                    jnp.maximum(a, sbuf[g, m, r * 8 : (r + 1) * 8, c * 128 : (c + 1) * 128] - col)
                    for c, a in enumerate(acc)
                )
            return acc

        start = tuple(jnp.full((8, 128), NEG_FILL, jnp.float32) for c in range(2 * keys // 128))
        acc = lax.fori_loop(0, group, member, start)
        best = jnp.concatenate([jnp.max(a, axis=0, keepdims=True) for a in acc], axis=1) * scale
        best = jnp.where(bias_of(g) < 0.0, NEG_FILL, best)
        cm[2 * g] = best[:, :keys]
        cm[2 * g + 1] = best[:, keys:]
        return unused

    lax.fori_loop(0, 2, best_pair, 0)

    place = z // 2 * NY + y

    def owner(step, unused):
        far, far_y = turn(slot, step // NY), turn(y, lax.rem(step, NY))
        remote(cm.at[far], rbuf.at[place], cs.at[0], cr.at[0], {"ctx": (HALF * side + far) * NX + x, "qry": far_y}).start()
        return unused

    lax.fori_loop(1, HALF * NY, owner, 0)

    @pl.when(inside)
    def _():
        pltpu.make_async_copy(cm.at[slot], rbuf.at[place], cr.at[0]).start()

    @pl.when(~inside)
    def _():
        owner(0, 0)

    drain(rbuf, cr.at[0])
    o_ref[...] = jnp.max(rbuf[...], axis=0)

    drain(sbuf.at[0, 0, pl.ds(0, 56)], ss.at[0])
    drain(colb.at[pl.ds(0, 7), pl.ds(0, 112)], qs.at[0])
    drain(kbuf.at[pl.ds(0, 3)], ys.at[0])

    @pl.when(inside)
    def _():
        drain(rbuf.at[pl.ds(0, HALF * NY - 1)], cs.at[0])
        drain(kbuf.at[0, pl.ds(0, 3)], ks.at[0])
        drain(pbuf.at[pl.ds(0, 3)], ps.at[0])

    @pl.when(~inside)
    def _():
        drain(rbuf, cs.at[0])
        drain(kbuf.at[0], ks.at[0])
        drain(pbuf, ps.at[0])


def shards(queries, key_cache, key_positions, span_end):
    own, unused, lanes = queries.shape
    keys, width = key_cache.shape[1:]
    group = lanes // width
    rows = own * NX * 2
    dma = lambda n: pltpu.SemaphoreType.DMA((n,))
    return pl.pallas_call(
        functools.partial(kernel, group),
        out_shape=jax.ShapeDtypeStruct((1, keys), jnp.float32),
        in_specs=[pl.BlockSpec(memory_space=pl.ANY)] * 4,
        out_specs=pl.BlockSpec(memory_space=pltpu.VMEM),
        scratch_shapes=[
            pltpu.VMEM((2, NX, own, lanes), jnp.bfloat16),
            pltpu.VMEM((NY, HALF, keys // NY, width), jnp.bfloat16),
            pltpu.VMEM((HALF, 1, keys), jnp.int32),
            pltpu.VMEM((1, own), jnp.int32),
            pltpu.VMEM((2, group, rows, 2 * keys), jnp.float32),
            pltpu.VMEM((group, rows, 128), jnp.float32),
            pltpu.VMEM((group, rows, 128), jnp.float32),
            pltpu.VMEM((group, rows, 128), jnp.float32),
            pltpu.VMEM((2, NX, 2, 16, 128), jnp.float32),
            pltpu.VMEM((HALF, 1, keys), jnp.float32),
            pltpu.VMEM((HALF * NY, 1, keys), jnp.float32),
            dma(1), dma(1), dma(2), dma(1), dma(1), dma(2), dma(1), dma(1), dma(1), dma(2), dma(1), dma(1), dma(1), dma(1), dma(1),
        ],
        compiler_params=pltpu.CompilerParams(collective_id=0, has_side_effects=True, vmem_limit_bytes=58 << 20),
    )(queries[:, 0], key_cache[0], key_positions[None], span_end[None])


def solution(mesh):
    placed = (P(("qry", "ctx"), "head", None), P("head", "ctx", None), P("ctx"), P(("qry", "ctx")))
    return jax.shard_map(shards, mesh=mesh, in_specs=placed, out_specs=P("head", "ctx"), check_vma=False)
```

time: 51.9 us -> 39.5 us (0.76)
  the two profiles are of different devices: /device:TPU:480 before, /device:TPU:6 now
where the time goes in v2:
time: 39.5 us; the launch traced here: 38.7 us
  Pallas kernels  37.5 us (95%)
  local copies, waits for them, and re-layouts  1.24 us (3%)
    pallas_call x1, Pallas kernels, shards(): pl.pallas_call(functools.partial(kernel, group), out_shape=jax.ShapeDtype...  37.5 us
    unnamed x1, local copies, waits for them, and re-layouts  1.24 us

profile of v2, /device:TPU:6, one launch (start us, length us, event | category | flops | bytes accessed | tf_op | source)
XLA Modules:
  0.0 38.7 jit_solution(2889676402176313298)
XLA Ops:
  0.0 37.5 %shard_map.46 = f32[1,256]{1,0:T(1,128)} custom-call(bf16[32,896]{1,0:T(8,128)(2,1)} %bitcast.5, bf16[256,128]{1,0:T(8,128)(2,1)} %bitcast.4, s32[1,256]{1,0:T(1,128)} %bitcast.6, s32[1,32]{1,0:T(1,128)} %bitcast.7), custom_call_target="tpu_custom_call" | custom-call | tf_op jit(solution)/shard_map/pallas_call | solution.py:226
  37.5 1.2 %copy.6 = f32[1,256]{1,0:T(1,128)} copy(f32[1,256]{1,0:T(1,128)} %shard_map.46) | data formatting | bytes 2048

commit v3 on v2

--- a/solution.py
+++ b/solution.py
@@ -15,7 +15,7 @@
 
 
 def kernel(group, q_ref, k_ref, p_ref, e_ref, o_ref, qbuf, kbuf, pbuf, ebuf, sbuf, mst, lst, colb, st, cm, rbuf,
-           lq, le, qr, qz, qs, kr, pr, ks, ps, yr, ys, ss, sr, cs, cr):
+           lq, le, qr, qz, qs, kr, pr, ks, ps, yr, ys, ss, sr, cs, cr, ready):
     ctx, y = lax.axis_index("ctx"), lax.axis_index("qry")
     z, x = ctx // NX, lax.rem(ctx, NX)
     side = lax.rem(z, 2)
@@ -47,16 +47,61 @@
         pl.semaphore_signal(barrier, inc=1, device_id=dev, device_id_type=MESH)
 
     for j in range(HALF):
+        source, target = HALF * side + j, 2 * j + half
+
+        @pl.when(source > z)
+        def _():
+            greet(at(source, x))
+
+        @pl.when(target > z)
+        def _():
+            greet(at(target, x))
+
+    for v in range(1, 4):
+
+        @pl.when(v > y)
+        def _():
+            greet({"qry": v})
+
+        @pl.when(v > x)
+        def _():
+            greet(at(z, v))
+
+    @pl.when(twin > z)
+    def _():
+        greet(at(twin, x))
+
+    lower = jnp.clip(z - HALF * side, 0, HALF) + (z - half + 1) // 2
+    waits = lower + x + y + side
+
+    @pl.when(waits > 0)
+    def _():
+        pl.semaphore_wait(barrier, waits)
+
+
+    def tell(index, dev):
+        pl.semaphore_signal(ready.at[index], inc=1, device_id=dev, device_id_type=MESH)
+
+    for j in range(HALF):
         source = HALF * side + j
 
-        @pl.when(source != z)
-        def _():
-            greet(at(source, x))
-
-    for d in (1, 3, 2):
-        greet({"qry": turn(y, d)})
-        greet(at(z, turn(x, d)))
-    greet(at(twin, x))
+        @pl.when(source < z)
+        def _():
+            tell(9 + z // 2, at(source, x))
+
+    @pl.when(side == 1)
+    def _():
+        tell(8, at(twin, x))
+
+    for v in range(3):
+
+        @pl.when(v < x)
+        def _():
+            tell(x, at(z, v))
+
+        @pl.when(v < y)
+        def _():
+            tell(4 + y, {"qry": v})
 
     pltpu.make_async_copy(q_ref, qbuf.at[side, x], lq.at[0]).start()
     pltpu.make_async_copy(e_ref, ebuf, le.at[0]).start()
@@ -70,23 +115,67 @@
     mst[...] = jnp.full(mst.shape, NEG_FILL, jnp.float32)
     lst[...] = jnp.zeros(lst.shape, jnp.float32)
     st[side, x] = jnp.zeros(st.shape[2:], jnp.float32)
-    pl.semaphore_wait(barrier, jnp.where(inside, 10, 11))
-
-    remote(q_ref, qbuf.at[side, x], qs.at[0], qz.at[0], at(twin, x)).start()
+    def send_keys(target):
+        remote(k_ref.at[mine], kbuf.at[y, slot], ks.at[0], kr.at[slot // 2], at(target, x)).start()
+        remote(p_ref, pbuf.at[slot], ps.at[0], pr.at[0], at(target, x)).start()
+
     for i in range(HALF):
         target = 2 * i + half
 
-        @pl.when(target != z)
-        def _():
-            remote(k_ref.at[mine], kbuf.at[y, slot], ks.at[0], kr.at[slot // 2], at(target, x)).start()
-            remote(p_ref, pbuf.at[slot], ps.at[0], pr.at[0], at(target, x)).start()
-
+        @pl.when(target < z)
+        def _():
+            send_keys(target)
+
+    right, left = turn(x, 1), turn(x, 3)
+
+    def send_twin():
+        remote(q_ref, qbuf.at[side, x], qs.at[0], qz.at[0], at(twin, x)).start()
+
+    pl.when(side == 1)(send_twin)
+    for v in range(NX):
+        if v:
+
+            @pl.when(v > x)
+            def _():
+                pl.semaphore_wait(ready.at[v], 1)
+
+        for index, near in ((0, right), (1, left)):
+
+            @pl.when(v == near)
+            def _():
+                remote(q_ref, qbuf.at[side, x], qs.at[0], qr.at[index], at(z, v)).start()
+
+    @pl.when(side == 0)
+    def _():
+        pl.semaphore_wait(ready.at[8], 1)
+        send_twin()
+
+    def send_later(near):
+        for i in range(HALF):
+            target = 2 * i + half
+
+            @pl.when((target > z) & ((target <= z + 2) if near else (target > z + 2)))
+            def _():
+                pl.semaphore_wait(ready.at[9 + i], 1)
+                send_keys(target)
+
+    send_later(True)
+
+    def forward(block, index, device):
+        remote(block, block, qs.at[0], qr.at[index], at(z, device)).start()
+
+    drain(q_ref, qr.at[1])
+    forward(qbuf.at[side, right], 2, left)
+    drain(q_ref, qz.at[0])
     for d in (1, 3, 2):
-        remote(q_ref, qbuf.at[side, x], qs.at[0], qr.at[0], at(z, turn(x, d))).start()
-    drain(qbuf.at[0, 0], qz.at[0])
-    passed = qbuf.at[1 - side, x]
-    for d in (1, 3, 2):
-        remote(passed, passed, qs.at[0], qr.at[1], at(z, turn(x, d))).start()
+        forward(qbuf.at[1 - side, x], 3, turn(x, d))
+    send_later(False)
+
+    for v in range(1, NY):
+
+        @pl.when(v > y)
+        def _():
+            pl.semaphore_wait(ready.at[4 + v], 1)
 
     def fan_out(g):
         drain(kbuf.at[0, pl.ds(0, 2)], kr.at[g])
@@ -94,11 +183,14 @@
         for d in (1, 3, 2):
             remote(part, part, ys.at[0], yr.at[g], {"qry": turn(y, d)}).start()
 
-    fan_out(0)
+    flip = jnp.where((z == 4) | (z >= 6), 1, 0)
+    fan_out(flip)
+    fan_out(1 - flip)
     drain(q_ref, lq.at[0])
     drain(e_ref, le.at[0])
-    drain(qbuf.at[0, pl.ds(0, NX - 1)], qr.at[0])
-    drain(qbuf.at[0, pl.ds(0, NX - 1)], qr.at[1])
+    drain(q_ref, qr.at[0])
+    drain(q_ref, qr.at[2])
+    drain(qbuf.at[0, pl.ds(0, NX - 1)], qr.at[3])
     drain(pbuf, pr.at[0])
     end = ebuf[0:1, 0:1]
 
@@ -106,10 +198,8 @@
         pos = jnp.concatenate([pbuf[2 * g], pbuf[2 * g + 1]], axis=1)
         return jnp.where(pos < end, 0.0, NEG_FILL)
 
-    def scan_pair(g, unused):
-        @pl.when(g < 1)
-        def _():
-            fan_out(g + 1)
+    def scan_pair(step, unused):
+        g = jnp.where(step == 0, flip, 1 - flip)
 
         drain(kbuf.at[pl.ds(0, NY - 1), pl.ds(0, 2)], yr.at[g])
         parts = [kbuf[:, 2 * g + j].reshape(keys, width) for j in range(2)]
@@ -140,19 +230,18 @@
             top = jnp.max(tops, axis=1, keepdims=True)
             mass = jnp.sum(lst[m, b * 128 : (b + 1) * 128] * jnp.exp2((tops - top) * to_exp2), axis=1, keepdims=True)
             r = m * (rows // 128) + b
-            st[side, x, 0, r : r + 1] = jnp.sum(jnp.where(eye, top, 0.0), axis=0, keepdims=True)
-            st[side, x, 1, r : r + 1] = jnp.sum(jnp.where(eye, mass, 0.0), axis=0, keepdims=True)
+            level = top + jnp.log(mass) * (1.0 / scale)
+            st[side, x, r : r + 1] = jnp.sum(jnp.where(eye, level, 0.0), axis=0, keepdims=True)
     own = st.at[side, x]
     for zz in (twin, z):
         for d in (2, 1, 3):
             remote(own, own, ss.at[0], sr.at[0], at(zz, turn(x, d))).start()
     remote(own, own, ss.at[0], sr.at[0], at(twin, x)).start()
 
-    drain(sbuf.at[0, 0, pl.ds(0, 56)], sr.at[0])
-    tops = [st[e, i, 0] for e in range(2) for i in range(NX)]
-    masses = [st[e, i, 1] for e in range(2) for i in range(NX)]
-    top = functools.reduce(jnp.maximum, tops)
-    mass = sum(b * jnp.exp2((a - top) * to_exp2) for a, b in zip(tops, masses))
+    drain(sbuf.at[0, 0, pl.ds(0, 56), pl.ds(0, 256)], sr.at[0])
+    levels = [st[e, i] for e in range(2) for i in range(NX)]
+    top = functools.reduce(jnp.maximum, levels)
+    mass = sum(jnp.exp2((a - top) * to_exp2) for a in levels)
     total = top + jnp.log(mass) * (1.0 / scale)
     for m in range(group):
         for b in range(rows // 128):
@@ -182,25 +271,23 @@
 
     place = z // 2 * NY + y
 
-    def owner(step, unused):
-        far, far_y = turn(slot, step // NY), turn(y, lax.rem(step, NY))
-        remote(cm.at[far], rbuf.at[place], cs.at[0], cr.at[0], {"ctx": (HALF * side + far) * NX + x, "qry": far_y}).start()
-        return unused
-
-    lax.fori_loop(1, HALF * NY, owner, 0)
+    for far in range(HALF):
+        owner = HALF * side + far
+        for d in range(NY):
+            send = lambda: remote(cm.at[far], rbuf.at[place], cs.at[0], cr.at[0], {"ctx": owner * NX + x, "qry": turn(y, d)}).start()
+            if d:
+                send()
+            else:
+                pl.when(owner != z)(send)
 
     @pl.when(inside)
     def _():
         pltpu.make_async_copy(cm.at[slot], rbuf.at[place], cr.at[0]).start()
-
-    @pl.when(~inside)
-    def _():
-        owner(0, 0)
 
     drain(rbuf, cr.at[0])
     o_ref[...] = jnp.max(rbuf[...], axis=0)
 
-    drain(sbuf.at[0, 0, pl.ds(0, 56)], ss.at[0])
+    drain(sbuf.at[0, 0, pl.ds(0, 56), pl.ds(0, 256)], ss.at[0])
     drain(colb.at[pl.ds(0, 7), pl.ds(0, 112)], qs.at[0])
     drain(kbuf.at[pl.ds(0, 3)], ys.at[0])
 
@@ -223,7 +310,7 @@
     group = lanes // width
     rows = own * NX * 2
     dma = lambda n: pltpu.SemaphoreType.DMA((n,))
-    return pl.pallas_call(
+    best = pl.pallas_call(
         functools.partial(kernel, group),
         out_shape=jax.ShapeDtypeStruct((1, keys), jnp.float32),
         in_specs=[pl.BlockSpec(memory_space=pl.ANY)] * 4,
@@ -237,13 +324,14 @@
             pltpu.VMEM((group, rows, 128), jnp.float32),
             pltpu.VMEM((group, rows, 128), jnp.float32),
             pltpu.VMEM((group, rows, 128), jnp.float32),
-            pltpu.VMEM((2, NX, 2, 16, 128), jnp.float32),
+            pltpu.VMEM((2, NX, 16, 128), jnp.float32),
             pltpu.VMEM((HALF, 1, keys), jnp.float32),
             pltpu.VMEM((HALF * NY, 1, keys), jnp.float32),
-            dma(1), dma(1), dma(2), dma(1), dma(1), dma(2), dma(1), dma(1), dma(1), dma(2), dma(1), dma(1), dma(1), dma(1), dma(1),
+            dma(1), dma(1), dma(4), dma(1), dma(1), dma(2), dma(1), dma(1), dma(1), dma(2), dma(1), dma(1), dma(1), dma(1), dma(1), pltpu.SemaphoreType.REGULAR((13,)),
         ],
         compiler_params=pltpu.CompilerParams(collective_id=0, has_side_effects=True, vmem_limit_bytes=58 << 20),
     )(queries[:, 0], key_cache[0], key_positions[None], span_end[None])
+    return best
 
 
 def solution(mesh):

time: 39.5 us -> 38.7 us (0.980); the launches traced: 38.7 us -> 38.6 us
  no operation moved by 1% of the time
where the time goes in v3:
time: 38.7 us; the launch traced here: 38.6 us
  Pallas kernels  37.3 us (96%)
  local copies, waits for them, and re-layouts  1.24 us (3%)
    pallas_call x1, Pallas kernels, shards(): pl.pallas_call(functools.partial(kernel, group), out_shape=jax.ShapeDtype...  37.3 us
    unnamed x1, local copies, waits for them, and re-layouts  1.24 us

profile of v3, /device:TPU:6, one launch (start us, length us, event | category | flops | bytes accessed | tf_op | source)
XLA Modules:
  0.0 38.6 jit_solution(15519072817931592644)
XLA Ops:
  0.0 37.3 %shard_map.46 = f32[1,256]{1,0:T(1,128)} custom-call(bf16[32,896]{1,0:T(8,128)(2,1)} %bitcast.5, bf16[256,128]{1,0:T(8,128)(2,1)} %bitcast.4, s32[1,256]{1,0:T(1,128)} %bitcast.6, s32[1,32]{1,0:T(1,128)} %bitcast.7), custom_call_target="tpu_custom_call" | custom-call | tf_op jit(solution)/shard_map/pallas_call | solution.py:313
  37.3 1.2 %copy.6 = f32[1,256]{1,0:T(1,128)} copy(f32[1,256]{1,0:T(1,128)} %shard_map.46) | data formatting | bytes 2048

commit v4 on v3

--- a/solution.py
+++ b/solution.py
@@ -223,15 +223,12 @@
 
     lax.fori_loop(0, 2, scan_pair, 0)
 
-    eye = lax.broadcasted_iota(jnp.int32, (128, 128), 0) == lax.broadcasted_iota(jnp.int32, (128, 128), 1)
-    for m in range(group):
-        for b in range(rows // 128):
-            tops = mst[m, b * 128 : (b + 1) * 128]
-            top = jnp.max(tops, axis=1, keepdims=True)
-            mass = jnp.sum(lst[m, b * 128 : (b + 1) * 128] * jnp.exp2((tops - top) * to_exp2), axis=1, keepdims=True)
-            r = m * (rows // 128) + b
-            level = top + jnp.log(mass) * (1.0 / scale)
-            st[side, x, r : r + 1] = jnp.sum(jnp.where(eye, level, 0.0), axis=0, keepdims=True)
+    blocks = [(m, b, m * (rows // 128) + b) for m in range(group) for b in range(rows // 128)]
+    for m, b, r in blocks:
+        tops, masses = mst[m, b * 128 : (b + 1) * 128].T, lst[m, b * 128 : (b + 1) * 128].T
+        top = jnp.max(tops, axis=0, keepdims=True)
+        mass = jnp.sum(masses * jnp.exp2((tops - top) * to_exp2), axis=0, keepdims=True)
+        st[side, x, r : r + 1] = top + jnp.log(mass) * (1.0 / scale)
     own = st.at[side, x]
     for zz in (twin, z):
         for d in (2, 1, 3):
@@ -243,11 +240,8 @@
     top = functools.reduce(jnp.maximum, levels)
     mass = sum(jnp.exp2((a - top) * to_exp2) for a in levels)
     total = top + jnp.log(mass) * (1.0 / scale)
-    for m in range(group):
-        for b in range(rows // 128):
-            r = m * (rows // 128) + b
-            col = jnp.sum(jnp.where(eye, total[r : r + 1], 0.0), axis=1, keepdims=True)
-            colb[m, b * 128 : (b + 1) * 128] = jnp.broadcast_to(col, (128, 128))
+    for m, b, r in blocks:
+        colb[m, b * 128 : (b + 1) * 128] = jnp.broadcast_to(total[r : r + 1], (128, 128)).T
 
     def best_pair(g, unused):
         def member(m, acc):

time: 38.7 us -> 38.2 us (0.987)
  Pallas kernels: 37.3 us -> 36.9 us
    pallas_call x1, Pallas kernels: 37.3 us -> 36.9 us  [shards(): pl.pallas_call(functools.partial(kernel, group), out_shape=jax.ShapeDtype...]
where the time goes in v4:
time: 38.2 us; the launch traced here: 38.1 us
  Pallas kernels  36.9 us (97%)
  local copies, waits for them, and re-layouts  1.24 us (3%)
    pallas_call x1, Pallas kernels, shards(): pl.pallas_call(functools.partial(kernel, group), out_shape=jax.ShapeDtype...  36.9 us
    unnamed x1, local copies, waits for them, and re-layouts  1.24 us

profile of v4, /device:TPU:6, one launch (start us, length us, event | category | flops | bytes accessed | tf_op | source)
XLA Modules:
  0.0 38.1 jit_solution(14804046104931608006)
XLA Ops:
  0.0 36.9 %shard_map.46 = f32[1,256]{1,0:T(1,128)} custom-call(bf16[32,896]{1,0:T(8,128)(2,1)} %bitcast.5, bf16[256,128]{1,0:T(8,128)(2,1)} %bitcast.4, s32[1,256]{1,0:T(1,128)} %bitcast.6, s32[1,32]{1,0:T(1,128)} %bitcast.7), custom_call_target="tpu_custom_call" | custom-call | tf_op jit(solution)/shard_map/pallas_call | solution.py:307
  36.9 1.2 %copy.6 = f32[1,256]{1,0:T(1,128)} copy(f32[1,256]{1,0:T(1,128)} %shard_map.46) | data formatting | bytes 2048

commit v5 on v4

--- a/solution.py
+++ b/solution.py
@@ -112,9 +112,6 @@
         pltpu.make_async_copy(k_ref.at[mine], kbuf.at[y, slot], kr.at[slot // 2]).start()
         pltpu.make_async_copy(p_ref, pbuf.at[slot], pr.at[0]).start()
 
-    mst[...] = jnp.full(mst.shape, NEG_FILL, jnp.float32)
-    lst[...] = jnp.zeros(lst.shape, jnp.float32)
-    st[side, x] = jnp.zeros(st.shape[2:], jnp.float32)
     def send_keys(target):
         remote(k_ref.at[mine], kbuf.at[y, slot], ks.at[0], kr.at[slot // 2], at(target, x)).start()
         remote(p_ref, pbuf.at[slot], ps.at[0], pr.at[0], at(target, x)).start()
@@ -183,6 +180,9 @@
         for d in (1, 3, 2):
             remote(part, part, ys.at[0], yr.at[g], {"qry": turn(y, d)}).start()
 
+    mst[...] = jnp.full(mst.shape, NEG_FILL, jnp.float32)
+    lst[...] = jnp.zeros(lst.shape, jnp.float32)
+    st[side, x] = jnp.zeros(st.shape[2:], jnp.float32)
     flip = jnp.where((z == 4) | (z >= 6), 1, 0)
     fan_out(flip)
     fan_out(1 - flip)
@@ -243,6 +243,8 @@
     for m, b, r in blocks:
         colb[m, b * 128 : (b + 1) * 128] = jnp.broadcast_to(total[r : r + 1], (128, 128)).T
 
+    place = z // 2 * NY + y
+
     def best_pair(g, unused):
         def member(m, acc):
             for r in range(rows // 8):
@@ -259,20 +261,19 @@
         best = jnp.where(bias_of(g) < 0.0, NEG_FILL, best)
         cm[2 * g] = best[:, :keys]
         cm[2 * g + 1] = best[:, keys:]
+        for j in range(2):
+            far = 2 * g + j
+            owner = HALF * side + far
+            for d in range(NY):
+                send = lambda: remote(cm.at[far], rbuf.at[place], cs.at[0], cr.at[0], {"ctx": owner * NX + x, "qry": turn(y, d)}).start()
+                if d:
+                    send()
+                else:
+                    pl.when(owner != z)(send)
         return unused
 
     lax.fori_loop(0, 2, best_pair, 0)
 
-    place = z // 2 * NY + y
-
-    for far in range(HALF):
-        owner = HALF * side + far
-        for d in range(NY):
-            send = lambda: remote(cm.at[far], rbuf.at[place], cs.at[0], cr.at[0], {"ctx": owner * NX + x, "qry": turn(y, d)}).start()
-            if d:
-                send()
-            else:
-                pl.when(owner != z)(send)
 
     @pl.when(inside)
     def _():

time: 38.2 us -> 37.9 us (level)
  Pallas kernels: 36.9 us -> 36.5 us
where the time goes in v5:
time: 37.9 us; the launch traced here: 37.8 us
  Pallas kernels  36.5 us (96%)
  local copies, waits for them, and re-layouts  1.24 us (3%)
    pallas_call x1, Pallas kernels, shards(): pl.pallas_call(functools.partial(kernel, group), out_shape=jax.ShapeDtype...  36.5 us
    unnamed x1, local copies, waits for them, and re-layouts  1.24 us

profile of v5, /device:TPU:6, one launch (start us, length us, event | category | flops | bytes accessed | tf_op | source)
XLA Modules:
  0.0 37.8 jit_solution(217140522508861642)
XLA Ops:
  0.0 36.5 %shard_map.46 = f32[1,256]{1,0:T(1,128)} custom-call(bf16[32,896]{1,0:T(8,128)(2,1)} %bitcast.5, bf16[256,128]{1,0:T(8,128)(2,1)} %bitcast.4, s32[1,256]{1,0:T(1,128)} %bitcast.6, s32[1,32]{1,0:T(1,128)} %bitcast.7), custom_call_target="tpu_custom_call" | custom-call | tf_op jit(solution)/shard_map/pallas_call | solution.py:308
  36.5 1.2 %copy.6 = f32[1,256]{1,0:T(1,128)} copy(f32[1,256]{1,0:T(1,128)} %shard_map.46) | data formatting | bytes 2048

commit v6 on v5

--- a/solution.py
+++ b/solution.py
@@ -14,8 +14,8 @@
 HALF = NZ // 2
 
 
-def kernel(group, q_ref, k_ref, p_ref, e_ref, o_ref, qbuf, kbuf, pbuf, ebuf, sbuf, mst, lst, colb, st, cm, rbuf,
-           lq, le, qr, qz, qs, kr, pr, ks, ps, yr, ys, ss, sr, cs, cr, ready):
+def kernel(group, q_ref, k_ref, p_ref, e_ref, o_ref, qbuf, kbuf, pbuf, ebuf, sbuf, mst, lst, colb, st, cm, rbuf, kown,
+           lk, lq, le, qr, qz, qs, kr, pr, ks, ps, yr, ys, ss, sr, cs, cr, ready):
     ctx, y = lax.axis_index("ctx"), lax.axis_index("qry")
     z, x = ctx // NX, lax.rem(ctx, NX)
     side = lax.rem(z, 2)
@@ -105,6 +105,7 @@
 
     pltpu.make_async_copy(q_ref, qbuf.at[side, x], lq.at[0]).start()
     pltpu.make_async_copy(e_ref, ebuf, le.at[0]).start()
+    pltpu.make_async_copy(k_ref.at[mine], kown, lk.at[0]).start()
     slot = lax.rem(z, HALF)
 
     @pl.when(inside)
@@ -112,8 +113,8 @@
         pltpu.make_async_copy(k_ref.at[mine], kbuf.at[y, slot], kr.at[slot // 2]).start()
         pltpu.make_async_copy(p_ref, pbuf.at[slot], pr.at[0]).start()
 
-    def send_keys(target):
-        remote(k_ref.at[mine], kbuf.at[y, slot], ks.at[0], kr.at[slot // 2], at(target, x)).start()
+    def send_keys(target, block):
+        remote(block, kbuf.at[y, slot], ks.at[0], kr.at[slot // 2], at(target, x)).start()
         remote(p_ref, pbuf.at[slot], ps.at[0], pr.at[0], at(target, x)).start()
 
     for i in range(HALF):
@@ -121,7 +122,7 @@
 
         @pl.when(target < z)
         def _():
-            send_keys(target)
+            send_keys(target, k_ref.at[mine])
 
     right, left = turn(x, 1), turn(x, 3)
 
@@ -154,8 +155,9 @@
             @pl.when((target > z) & ((target <= z + 2) if near else (target > z + 2)))
             def _():
                 pl.semaphore_wait(ready.at[9 + i], 1)
-                send_keys(target)
-
+                send_keys(target, kown)
+
+    drain(kown, lk.at[0])
     send_later(True)
 
     def forward(block, index, device):
@@ -322,7 +324,8 @@
             pltpu.VMEM((2, NX, 16, 128), jnp.float32),
             pltpu.VMEM((HALF, 1, keys), jnp.float32),
             pltpu.VMEM((HALF * NY, 1, keys), jnp.float32),
-            dma(1), dma(1), dma(4), dma(1), dma(1), dma(2), dma(1), dma(1), dma(1), dma(2), dma(1), dma(1), dma(1), dma(1), dma(1), pltpu.SemaphoreType.REGULAR((13,)),
+            pltpu.VMEM((keys // NY, width), jnp.bfloat16),
+            dma(1), dma(1), dma(1), dma(4), dma(1), dma(1), dma(2), dma(1), dma(1), dma(1), dma(2), dma(1), dma(1), dma(1), dma(1), dma(1), pltpu.SemaphoreType.REGULAR((13,)),
         ],
         compiler_params=pltpu.CompilerParams(collective_id=0, has_side_effects=True, vmem_limit_bytes=58 << 20),
     )(queries[:, 0], key_cache[0], key_positions[None], span_end[None])

time: 37.9 us -> 37.8 us (level)
  no operation moved by 1% of the time
where the time goes in v6:
time: 37.8 us; the launch traced here: 37.6 us
  Pallas kernels  36.3 us (96%)
  local copies, waits for them, and re-layouts  1.24 us (3%)
    pallas_call x1, Pallas kernels, shards(): pl.pallas_call(functools.partial(kernel, group), out_shape=jax.ShapeDtype...  36.3 us
    unnamed x1, local copies, waits for them, and re-layouts  1.24 us

profile of v6, /device:TPU:6, one launch (start us, length us, event | category | flops | bytes accessed | tf_op | source)
XLA Modules:
  0.0 37.6 jit_solution(17895362056951787418)
XLA Ops:
  0.0 36.3 %shard_map.46 = f32[1,256]{1,0:T(1,128)} custom-call(bf16[32,896]{1,0:T(8,128)(2,1)} %bitcast.5, bf16[256,128]{1,0:T(8,128)(2,1)} %bitcast.4, s32[1,256]{1,0:T(1,128)} %bitcast.6, s32[1,32]{1,0:T(1,128)} %bitcast.7), custom_call_target="tpu_custom_call" | custom-call | tf_op jit(solution)/shard_map/pallas_call | solution.py:310
  36.3 1.2 %copy.6 = f32[1,256]{1,0:T(1,128)} copy(f32[1,256]{1,0:T(1,128)} %shard_map.46) | data formatting | bytes 2048

commit v7 on v6

--- a/solution.py
+++ b/solution.py
@@ -182,8 +182,6 @@
         for d in (1, 3, 2):
             remote(part, part, ys.at[0], yr.at[g], {"qry": turn(y, d)}).start()
 
-    mst[...] = jnp.full(mst.shape, NEG_FILL, jnp.float32)
-    lst[...] = jnp.zeros(lst.shape, jnp.float32)
     st[side, x] = jnp.zeros(st.shape[2:], jnp.float32)
     flip = jnp.where((z == 4) | (z >= 6), 1, 0)
     fan_out(flip)
@@ -200,8 +198,8 @@
         pos = jnp.concatenate([pbuf[2 * g], pbuf[2 * g + 1]], axis=1)
         return jnp.where(pos < end, 0.0, NEG_FILL)
 
-    def scan_pair(step, unused):
-        g = jnp.where(step == 0, flip, 1 - flip)
+    def scan_pair(step):
+        g = 1 - flip if step else flip
 
         drain(kbuf.at[pl.ds(0, NY - 1), pl.ds(0, 2)], yr.at[g])
         parts = [kbuf[:, 2 * g + j].reshape(keys, width) for j in range(2)]
@@ -214,16 +212,19 @@
                 sbuf[g, m, :, j * keys : (j + 1) * keys] = s
                 t = s + bias[:, j * keys : (j + 1) * keys]
                 pieces += [t[:, c * 128 : (c + 1) * 128] for c in range(keys // 128)]
-            old = mst[m]
-            new = functools.reduce(jnp.maximum, pieces, old)
-            total = lst[m] * jnp.exp2((old - new) * to_exp2)
+            if step:
+                new = functools.reduce(jnp.maximum, pieces, mst[m])
+                total = lst[m] * jnp.exp2((mst[m] - new) * to_exp2)
+            else:
+                new = functools.reduce(jnp.maximum, pieces)
+                total = jnp.zeros_like(new)
             for piece in pieces:
                 total = total + jnp.exp2((piece - new) * to_exp2)
             mst[m] = new
             lst[m] = total
-        return unused
-
-    lax.fori_loop(0, 2, scan_pair, 0)
+
+    for step in range(2):
+        scan_pair(step)
 
     blocks = [(m, b, m * (rows // 128) + b) for m in range(group) for b in range(rows // 128)]
     for m, b, r in blocks:

time: 37.8 us -> 37.3 us (0.987)
  Pallas kernels: 36.3 us -> 35.9 us
    pallas_call x1, Pallas kernels: 36.3 us -> 35.9 us  [shards(): pl.pallas_call(functools.partial(kernel, group), out_shape=jax.ShapeDtype...]
where the time goes in v7:
time: 37.3 us; the launch traced here: 37.1 us
  Pallas kernels  35.9 us (96%)
  local copies, waits for them, and re-layouts  1.24 us (3%)
    pallas_call x1, Pallas kernels, shards(): pl.pallas_call(functools.partial(kernel, group), out_shape=jax.ShapeDtype...  35.9 us
    unnamed x1, local copies, waits for them, and re-layouts  1.24 us

profile of v7, /device:TPU:6, one launch (start us, length us, event | category | flops | bytes accessed | tf_op | source)
XLA Modules:
  0.0 37.1 jit_solution(9206859410962806079)
XLA Ops:
  0.0 35.9 %shard_map.46 = f32[1,256]{1,0:T(1,128)} custom-call(bf16[32,896]{1,0:T(8,128)(2,1)} %bitcast.5, bf16[256,128]{1,0:T(8,128)(2,1)} %bitcast.4, s32[1,256]{1,0:T(1,128)} %bitcast.6, s32[1,32]{1,0:T(1,128)} %bitcast.7), custom_call_target="tpu_custom_call" | custom-call | tf_op jit(solution)/shard_map/pallas_call | solution.py:311
  35.9 1.2 %copy.6 = f32[1,256]{1,0:T(1,128)} copy(f32[1,256]{1,0:T(1,128)} %shard_map.46) | data formatting | bytes 2048

commit v8 on v7

--- a/solution.py
+++ b/solution.py
@@ -275,7 +275,8 @@
                     pl.when(owner != z)(send)
         return unused
 
-    lax.fori_loop(0, 2, best_pair, 0)
+    for g in range(2):
+        best_pair(g, 0)
 
 
     @pl.when(inside)

time: 37.3 us -> 37.3 us (level)
  no operation moved by 1% of the time
where the time goes in v8:
time: 37.3 us; the launch traced here: 37.1 us
  Pallas kernels  35.9 us (96%)
  local copies, waits for them, and re-layouts  1.24 us (3%)
    pallas_call x1, Pallas kernels, shards(): pl.pallas_call(functools.partial(kernel, group), out_shape=jax.ShapeDtype...  35.9 us
    unnamed x1, local copies, waits for them, and re-layouts  1.24 us

profile of v8, /device:TPU:6, one launch (start us, length us, event | category | flops | bytes accessed | tf_op | source)
XLA Modules:
  0.0 37.1 jit_solution(11459586607623405645)
XLA Ops:
  0.0 35.9 %shard_map.46 = f32[1,256]{1,0:T(1,128)} custom-call(bf16[32,896]{1,0:T(8,128)(2,1)} %bitcast.5, bf16[256,128]{1,0:T(8,128)(2,1)} %bitcast.4, s32[1,256]{1,0:T(1,128)} %bitcast.6, s32[1,32]{1,0:T(1,128)} %bitcast.7), custom_call_target="tpu_custom_call" | custom-call | tf_op jit(solution)/shard_map/pallas_call | solution.py:312
  35.9 1.2 %copy.6 = f32[1,256]{1,0:T(1,128)} copy(f32[1,256]{1,0:T(1,128)} %shard_map.46) | data formatting | bytes 2048
